TPU v7x, 32 devices: a whole 2x2x4 slice. The times are simulated.
32 devices in a mesh: grp: 2 (over y), chan: 2 (over x), tm: 4 (over z), pol: 2 (over core).
Axes of the slice: x: 2, y: 2, z: 4, core: 2. Of those that a mesh axis runs over, the one named last changes fastest.
Arguments:
- voltages: bfloat16 [4, 2, 256, 32768], P('grp', 'pol', 'chan', 'tm'), parts along dimension 0, may hold values from -6 to 6
- taps_filter: float32 [16, 2048], replicated, may hold values from -1.5 to 1.5
- tile_a: int32 [14, 64], replicated, may hold values from 0 to 255
- tile_b: int32 [14, 64], replicated, may hold values from 0 to 255
- tile_owner: int32 [14], replicated, may hold values from 0 to 1, as said below
- tile_flags: int32 [14, 16], replicated, may hold values 0 or 1
Outputs:
- visibility: float32 [16, 256, 4, 2, 64, 128], P('pol', ('chan', 'tm'), 'grp'), parts along dimension 2
There are 2 independent parts, one for each index of `grp`. A program takes and returns all parts, laid end to end along the dimension named above; an argument that names none is the same for every part. Nothing has to cross between parts.
Inputs may be any that keep to these rules, and one draw needn't show every extreme that they name: `tile_owner`: one owner holds exactly 8 tiles and the other owner holds all the rest.
All inputs are finite; a program needn't handle non-finite values.
Results may differ from a plain program's by a relative error of at most 0.0035.
Values may be sent and summed in bfloat16 or wider, within the bound.
A program may use at most 128 MiB of HBM per device.

v0:
```python
import math
import jax
import jax.numpy as jnp
from jax import lax
from jax.sharding import PartitionSpec as P

AVG = 8
CAP = 8
radix_first = 32


def from_behind(value, axis, steps):
    count = lax.axis_size(axis)
    first, last = (max(0, -steps), min(count, count - steps))
    return lax.ppermute(value, axis, [(source, source + steps) for source in range(first, last)])


def fourier(filtered):
    length = filtered.shape[-1]
    second = length // radix_first
    exact_mode = lax.Precision.HIGHEST
    grid = filtered.reshape(filtered.shape[:-1] + (radix_first, second))
    outer = jnp.arange(radix_first, dtype=jnp.int32)
    inner = jnp.arange(second, dtype=jnp.int32)
    phase_one = (
        2.0
        * math.pi
        / radix_first
        * (outer[:, None] * outer[None, :] % radix_first).astype(jnp.float32)
    )
    phase_twist = 2.0 * math.pi / length * (outer[:, None] * inner[None, :]).astype(jnp.float32)
    phase_two = (
        2.0 * math.pi / second * (inner[:, None] * inner[None, :] % second).astype(jnp.float32)
    )
    cos_one, sin_one = (jnp.cos(phase_one), jnp.sin(phase_one))
    cos_twist, sin_twist = (jnp.cos(phase_twist), jnp.sin(phase_twist))
    cos_two, sin_two = (jnp.cos(phase_two), jnp.sin(phase_two))
    first_form = "fk,stkj->stfj"
    section_re = jnp.einsum(first_form, cos_one, grid[0], precision=exact_mode) + jnp.einsum(
        first_form, sin_one, grid[1], precision=exact_mode
    )
    section_im = jnp.einsum(first_form, cos_one, grid[1], precision=exact_mode) - jnp.einsum(
        first_form, sin_one, grid[0], precision=exact_mode
    )
    turned_re = section_re * cos_twist + section_im * sin_twist
    turned_im = section_im * cos_twist - section_re * sin_twist
    second_form = "gj,stfj->stgf"
    final_re = jnp.einsum(second_form, cos_two, turned_re, precision=exact_mode) + jnp.einsum(
        second_form, sin_two, turned_im, precision=exact_mode
    )
    final_im = jnp.einsum(second_form, cos_two, turned_im, precision=exact_mode) - jnp.einsum(
        second_form, sin_two, turned_re, precision=exact_mode
    )
    joined = jnp.stack([final_re, final_im]).reshape(filtered.shape)
    return joined * (1.0 / math.sqrt(length))


def correlate(full, rows_a, rows_b, flags, group_count):
    depth = full.shape[4]
    weight = jnp.tile(flags.astype(jnp.bfloat16), depth // flags.shape[0])
    left_rows = jnp.take(full, rows_a, axis=2) * weight
    right_rows = jnp.take(full, rows_b, axis=2)
    stacked_left = jnp.stack(
        [
            jnp.concatenate([left_rows[0], left_rows[1]], axis=-1),
            jnp.concatenate([left_rows[1], -left_rows[0]], axis=-1),
        ]
    )
    joined_right = jnp.concatenate([right_rows[0], right_rows[1]], axis=-1)
    result = jnp.einsum(
        "rpank,qbnk->nrpaqb", stacked_left, joined_right, preferred_element_type=jnp.float32
    )
    width = rows_a.shape[0]
    return result.reshape(group_count, 2, 2, width, 2 * width) * (1.0 / depth)


def on_device(voltages, taps_filter, tile_a, tile_b, tile_owner, tile_flags):
    history = taps_filter.shape[0] - 1
    length = taps_filter.shape[1]
    stations = voltages.shape[2]
    frames = voltages.shape[3] // length
    local_blocks = voltages.reshape(2, stations, frames, length)
    hop_count = -(-history // frames)
    sending = local_blocks
    extended = local_blocks
    for hop_index in range(hop_count):
        sending = from_behind(sending, "tm", 1)
        extended = jnp.concatenate([sending, extended], axis=2)
    extended = extended[:, :, extended.shape[2] - history - frames :]
    filtered = jnp.zeros((2, stations, frames, length), jnp.float32)
    for tap_index in range(history + 1):
        start = history - tap_index
        filtered = filtered + taps_filter[tap_index] * extended[
            :, :, start : start + frames
        ].astype(jnp.float32)
    spectra = fourier(filtered).astype(jnp.bfloat16)
    chan_count = lax.axis_size("chan")
    time_count = lax.axis_size("tm")
    narrow = length // (chan_count * time_count)
    outgoing = spectra.reshape(2, stations, frames, chan_count, time_count, narrow)
    outgoing = outgoing.transpose(0, 3, 4, 5, 1, 2)
    flat = outgoing.reshape(2, chan_count * time_count, narrow, stations * frames)
    moved = lax.all_to_all(flat, ("chan", "tm"), split_axis=1, concat_axis=1, tiled=True)
    moved = moved.reshape(2, chan_count, time_count, narrow, stations, frames)
    bands = narrow // AVG
    every_station = chan_count * stations
    spectra_count = time_count * frames
    arranged = moved.transpose(0, 1, 4, 3, 2, 5).reshape(
        2, 1, every_station, bands, AVG * spectra_count
    )
    full = lax.all_gather(arranged, "pol", axis=1, tiled=True)
    position = lax.axis_index("pol")
    width = tile_a.shape[1]
    capacity = CAP
    held = tile_owner == position
    listed = jnp.nonzero(held, size=capacity, fill_value=0)[0].astype(jnp.int32)
    tally = jnp.sum(held.astype(jnp.int32))
    initial = jnp.zeros((capacity, bands, 2, 2, width, 2 * width), jnp.float32)

    def fill_slot(slot, results):
        chosen_tile = listed[slot]
        return results.at[slot].set(
            correlate(
                full, tile_a[chosen_tile], tile_b[chosen_tile], tile_flags[chosen_tile], bands
            )
        )

    visibility = lax.fori_loop(0, tally, fill_slot, initial)
    return visibility


def solution(mesh):
    return jax.shard_map(
        on_device,
        mesh=mesh,
        in_specs=(P("grp", "pol", "chan", "tm"), P(), P(), P(), P(), P()),
        out_specs=P("pol", ("chan", "tm"), "grp", None, None, None),
        check_vma=False,
    )
```

profile of v0, /device:TPU:0, one launch (start us, length us, event | category | flops | bytes accessed | tf_op | source)
XLA Modules:
  0.0 1050.4 jit_solution(11831721690737286427)
XLA Ops:
  18.1 89.9 %collective-permute-done = bf16[2,128,4,2048]{1,3,2,0:T(8,128)(2,1)S(1)} collective-permute-done((bf16[2,128,4,2048]{1,3,2,0:T(8,128)(2,1)}, bf16[2,128,4,2048]{1,3,2,0:T(8,128)(2,1)S(1)}, u32[]{:S(2)}, u32[]{:S(2)}) %collective-permute-start) | collective-permute-done | bytes 4194336 | tf_op jit(solution)/shard_map/ppermute | solution.py:15
  112.5 88.7 %collective-permute-done.1 = bf16[2,128,4,2048]{1,3,2,0:T(8,128)(2,1)S(1)} collective-permute-done((bf16[2,128,4,2048]{1,3,2,0:T(8,128)(2,1)S(1)}, bf16[2,128,4,2048]{1,3,2,0:T(8,128)(2,1)S(1)}, u32[]{:S(2)}, u32[]{:S(2)}) %collective-permute-start.1) | collective-permute-done | bytes 4194336 | tf_op jit(solution)/shard_map/ppermute | solution.py:15
  205.8 87.8 %collective-permute-done.2 = bf16[2,128,4,2048]{1,3,2,0:T(8,128)(2,1)S(1)} collective-permute-done((bf16[2,128,4,2048]{1,3,2,0:T(8,128)(2,1)S(1)}, bf16[2,128,4,2048]{1,3,2,0:T(8,128)(2,1)S(1)}, u32[]{:S(2)}, u32[]{:S(2)}) %collective-permute-start.2) | collective-permute-done | bytes 4194336 | tf_op jit(solution)/shard_map/ppermute | solution.py:15
  298.5 86.6 %collective-permute-done.3 = bf16[2,128,4,2048]{1,3,2,0:T(8,128)(2,1)S(1)} collective-permute-done((bf16[2,128,4,2048]{1,3,2,0:T(8,128)(2,1)S(1)}, bf16[2,128,4,2048]{1,3,2,0:T(8,128)(2,1)S(1)}, u32[]{:S(2)}, u32[]{:S(2)}) %collective-permute-start.3) | collective-permute-done | bytes 4194336 | tf_op jit(solution)/shard_map/ppermute | solution.py:15
  402.7 24.3 %multiply_add_fusion = f32[2,128,4,2048]{1,3,2,0:T(8,128)} fusion(bf16[2,128,4,2048]{1,3,2,0:T(8,128)(2,1)} %copy-done.4, bf16[2,128,4,2048]{1,3,2,0:T(8,128)(2,1)S(1)} %collective-permute-done.1, bf16[2,128,4,2048]{1,3,2,0:T(8,128)(2,1)} %copy-done.5, bf16[2,128,4,2048]{1,3,2,0:T(8,128)(2,1)} %bitcast.161, bf16[2,128,8,2048]{1,3,2,0:T(8,128)(2,1)} %copy-done.2, ...), kind=kLoop, calls=%fused_computation.44 | loop fusion | flops 104857600 | bytes 63045632 | tf_op jit(solution)/shard_map/add | solution.py:93
  450.9 8.5 fusion.16
  494.1 11.2 %copy.62 = bf16[2,2,4,256,128,4]{3,0,5,4,2,1:T(2,128)(2,1)} copy(bf16[2,2,4,256,128,4]{4,3,2,1,5,0:T(8,128)(2,1)} %fusion.13) | data formatting | bytes 8388608 | tf_op jit(solution)/shard_map/transpose | solution.py:101
  505.4 97.2 %all_to_all.5 = bf16[2,8,256,512]{2,0,3,1:T(2,128)(2,1)} all-to-all(bf16[2,8,256,512]{2,0,3,1:T(2,128)(2,1)} %bitcast.158), channel_id=1, replica_groups=mesh['grp'=2,'chan'=2,'tm'=4,'pol'=2] {'chan','tm'}, dimensions={1} | all-to-all | bytes 8388608 | tf_op jit(solution)/shard_map/all_to_all | solution.py:103
  602.6 19.8 %copy.63 = bf16[2,2,128,256,4,4]{2,1,5,4,3,0:T(2,128)(2,1)} copy(bf16[2,2,128,256,4,4]{3,0,5,2,4,1:T(2,128)(2,1)} %bitcast.159) | data formatting | bytes 8388608 | tf_op jit(solution)/shard_map/transpose | solution.py:108
  630.0 7.8 copy.64
  641.1 14.2 %all-gather.2.cloned.1.call-done = bf16[2,2,256,32,128]{4,3,2,0,1:T(8,128)(2,1)} async-done(((bf16[2,1,256,32,128]{4,3,2,0,1:T(8,128)(2,1)}), bf16[2,2,256,32,128]{4,3,2,0,1:T(8,128)(2,1)}) %all-gather.2.cloned.1.call-update) | async-done | bytes 8388624 | tf_op jit(solution)/shard_map/all_gather | solution.py:111
  655.3 8.4 copy.65
  663.7 11.5 %broadcast_in_dim.13 = f32[8,32,2,2,64,128]{5,4,3,2,1,0:T(8,128)} broadcast(f32[]{:T(128)} %constant.110.clone.1), dimensions={} | broadcast | bytes 33554436 | tf_op jit(solution)/shard_map/broadcast_in_dim | solution.py:118
  675.2 368.1 %while.11 = (s32[]{:T(128)}, f32[8,32,2,2,64,128]{5,4,3,2,1,0:T(8,128)}, s32[]{:T(128)}, s32[8]{0:T(128)S(1)}, s32[14,64]{1,0:T(8,128)}, /*index=5*/bf16[2,2,256...) while((s32[]{:T(128)}, ...), condition=%wide.region_6.8_spmd, body=%wide.region_4.7_spmd.sunk | while | flops 563612416 | bytes 78656224 | solution.py:128
  704.8 8.8 mul.774
  742.9 7.8 copy.109
  750.7 8.8 mul.774
  788.8 7.8 copy.109
  796.6 8.8 mul.774
  842.5 8.8 mul.774
  888.5 8.8 mul.774
  934.4 8.8 mul.774
  980.3 8.8 mul.774
  1026.3 8.8 mul.774
  (223 shorter events, 371.4 us)
Async XLA Ops:
  6.5 291.8 %copy-start.6 = (f32[16,2048]{1,0:T(8,128)S(1)}, f32[16,2048]{1,0:T(8,128)}, u32[]{:S(2)}) copy-start(f32[16,2048]{1,0:T(8,128)} %param.13) | copy-start | bytes 393220
  6.5 648.8 %all-gather.2.cloned.1.call-start = ((), (), s32[]{:S(2)}) async-start(), calls=%async_computation.1 | async-start | bytes 12582912 | tf_op jit(solution)/shard_map/all_gather | solution.py:111
  12.9 95.1 %collective-permute-start = (bf16[2,128,4,2048]{1,3,2,0:T(8,128)(2,1)}, bf16[2,128,4,2048]{1,3,2,0:T(8,128)(2,1)S(1)}, u32[]{:S(2)}, u32[]{:S(2)}) collective-permute-start(bf16[2,128,4,2048]{1,3,2,0:T(8,128)(2,1)} %bitcast.160), channel_id=1, source_target_pairs={{0,2},{2,4},{4,6},{1,3},{3,5},{5,7},{8,10},{10,12},{12,14},{9,11},... | collective-permute-start | bytes 12582920 | tf_op jit(solution)/shard_map/ppermute | solution.py:15
  108.0 185.6 %copy-start.5 = (bf16[2,128,4,2048]{1,3,2,0:T(8,128)(2,1)}, bf16[2,128,4,2048]{1,3,2,0:T(8,128)(2,1)S(1)}, u32[]{:S(2)}) copy-start(bf16[2,128,4,2048]{1,3,2,0:T(8,128)(2,1)S(1)} %collective-permute-done) | copy-start | bytes 12582916
  108.0 93.2 %collective-permute-start.1 = (bf16[2,128,4,2048]{1,3,2,0:T(8,128)(2,1)S(1)}, bf16[2,128,4,2048]{1,3,2,0:T(8,128)(2,1)S(1)}, u32[]{:S(2)}, u32[]{:S(2)}) collective-permute-start(bf16[2,128,4,2048]{1,3,2,0:T(8,128)(2,1)S(1)} %collective-permute-done), channel_id=1, source_target_pairs={{0,2},{2,4},{4,6},{1,3},{3,5},{5,7},{8,10},{10,12},{12,14},{9,11},... | collective-permute-start | bytes 12582920 | tf_op jit(solution)/shard_map/ppermute | solution.py:15
  201.2 92.4 %collective-permute-start.2 = (bf16[2,128,4,2048]{1,3,2,0:T(8,128)(2,1)S(1)}, bf16[2,128,4,2048]{1,3,2,0:T(8,128)(2,1)S(1)}, u32[]{:S(2)}, u32[]{:S(2)}) collective-permute-start(bf16[2,128,4,2048]{1,3,2,0:T(8,128)(2,1)S(1)} %collective-permute-done.1), channel_id=1, source_target_pairs={{0,2},{2,4},{4,6},{1,3},{3,5},{5,7},{8,10},{10,12},{12,14},{9,11},... | collective-permute-start | bytes 12582920 | tf_op jit(solution)/shard_map/ppermute | solution.py:15
  293.6 4.9 copy-start.4
  293.6 91.5 %collective-permute-start.3 = (bf16[2,128,4,2048]{1,3,2,0:T(8,128)(2,1)S(1)}, bf16[2,128,4,2048]{1,3,2,0:T(8,128)(2,1)S(1)}, u32[]{:S(2)}, u32[]{:S(2)}) collective-permute-start(bf16[2,128,4,2048]{1,3,2,0:T(8,128)(2,1)S(1)} %collective-permute-done.2), channel_id=1, source_target_pairs={{0,2},{2,4},{4,6},{1,3},{3,5},{5,7},{8,10},{10,12},{12,14},{9,11},... | collective-permute-start | bytes 12582920 | tf_op jit(solution)/shard_map/ppermute | solution.py:15
  388.9 3.4 copy-start.2
  393.6 5.8 copy-start
  399.4 3.2 copy-start.1
  637.8 0.7 copy-start.7
  663.7 11.5 %copy-start.8 = (s32[6]{0:T(128)S(1)}, s32[6]{0:T(128)}, u32[]{:S(2)}) copy-start(s32[6]{0:T(128)} %constant.105.clone.1) | copy-start | bytes 76
  694.3 1.2 copy-start.3
  740.2 1.2 copy-start.3
  786.1 1.2 copy-start.3
  832.0 1.2 copy-start.3
  878.0 1.2 copy-start.3
  923.9 1.2 copy-start.3
  969.8 1.2 copy-start.3
  1015.8 1.2 copy-start.3
Sparse Core Ops, SparseCore 0:
  637.9 17.3 all-gather.1
where the time goes:
time: 1060 us; the launch traced here: 1050 us
  waiting for transfers between devices  367 us (35%)
  local copies, waits for them, and re-layouts  324 us (31%)
  other arithmetic  139 us (13%)
  blocking collectives  97.2 us (9%)
  matrix products  67.4 us (6%)
  loops' own time  23 us (2%)
  starting transfers between devices  19 us (2%)
  between operations  13.9 us (1%)
    ppermute x4, waiting for transfers between devices, from_behind(): lax.ppermute(value, axis, [(source, source + steps) for source in range(f...  353 us
    mul x16, local copies, waits for them, and re-layouts, correlate(): return result.reshape(group_count, 2, 2, width, 2 * width) * (1.0 / depth)  133 us
    all_to_all x1, blocking collectives, on_device(): lax.all_to_all(flat, ('chan', 'tm'), split_axis=1, concat_axis=1, tiled=T...  97.2 us
    scatter x8, other arithmetic, fill_slot(): results.at[slot]  60.2 us
    gather x8, local copies, waits for them, and re-layouts, correlate(): right_rows = jnp.take(full, rows_b, axis=2)  34.7 us
    gather x8, local copies, waits for them, and re-layouts, correlate(): left_rows = jnp.take(full, rows_a, axis=2) * weight  34.6 us
    add x1, other arithmetic, on_device(): filtered + taps_filter[tap_index] * extended[:, :, start:start + frames]....  24.3 us
    another operation x1, loops' own time, on_device(): visibility = lax.fori_loop(0, tally, fill_slot, initial)  23 us
  transfers between devices with their start and end apart: 5, of which 5 were waited for; matrix products, arithmetic and copies ran while one was open for 0% of the time, Pallas kernels for 0%

commit v1 on v0

--- a/solution.py
+++ b/solution.py
@@ -7,6 +7,18 @@
 AVG = 8
 CAP = 8
 radix_first = 32
+
+
+def cut_along(array, dim, devices):
+    shape = array.shape
+    blocks = array.reshape(*shape[:dim], devices, shape[dim] // devices, *shape[dim + 1 :])
+    return jnp.moveaxis(blocks, dim, 0)
+
+
+def joined_along(tiles, dim):
+    shape = list(tiles.shape[1:])
+    shape[dim] *= tiles.shape[0]
+    return jnp.moveaxis(tiles, 0, dim).reshape(shape)
 
 
 def from_behind(value, axis, steps):
@@ -100,7 +112,17 @@
     outgoing = spectra.reshape(2, stations, frames, chan_count, time_count, narrow)
     outgoing = outgoing.transpose(0, 3, 4, 5, 1, 2)
     flat = outgoing.reshape(2, chan_count * time_count, narrow, stations * frames)
-    moved = lax.all_to_all(flat, ("chan", "tm"), split_axis=1, concat_axis=1, tiled=True)
+    size, index = (lax.axis_size(("chan", "tm")), lax.axis_index(("chan", "tm")))
+    tiles = cut_along(flat, 1, size)
+    out = tiles
+    for turn in range(1, size):
+        target, source_2 = ((index + turn) % size, (index - turn) % size)
+        sent = lax.dynamic_index_in_dim(tiles, target, 0)
+        partner_block = lax.ppermute(
+            sent, ("chan", "tm"), [(i, (i + turn) % size) for i in range(size)]
+        )
+        out = lax.dynamic_update_slice_in_dim(out, partner_block, source_2, axis=0)
+    moved = joined_along(out, 1)
     moved = moved.reshape(2, chan_count, time_count, narrow, stations, frames)
     bands = narrow // AVG
     every_station = chan_count * stations

time: 1060 us -> 1070 us (level)
  blocking collectives: 97.2 us -> 0 us
  starting transfers between devices: 19 us -> 82.5 us
  local copies, waits for them, and re-layouts: 324 us -> 346 us
  waiting for transfers between devices: 367 us -> 387 us
    all_to_all x1 -> x0, blocking collectives: 97.2 us -> none  [on_device(): lax.all_to_all(flat, ('chan', 'tm'), split_axis=1, concat_axis=1, tiled=T...]
    ppermute x0 -> x7, starting transfers between devices: none -> 59.9 us  [on_device(): lax.ppermute(sent, ('chan', 'tm'), [(i, (i + turn) % size) for i in range...]
    ppermute x0 -> x7, waiting for transfers between devices: none -> 13.6 us  [on_device(): lax.ppermute(sent, ('chan', 'tm'), [(i, (i + turn) % size) for i in range...]
    dynamic_update_slice x0 -> x7, local copies, waits for them, and re-layouts: none -> 13.3 us  [on_device(): out = lax.dynamic_update_slice_in_dim(out, partner_block, source_2, axis=0)]
    unnamed x20 -> x22, local copies, waits for them, and re-layouts: 18.8 us -> 23.1 us
  transfers between devices with their start and end apart: 5 -> 12, of which waited for: 5 -> 8; matrix products, arithmetic and copies ran while one was open for 0% -> 1% of each run, Pallas kernels for 0% -> 0%
where the time goes in v1:
time: 1070 us; the launch traced here: 1060 us
  waiting for transfers between devices  387 us (36%)
  local copies, waits for them, and re-layouts  346 us (32%)
  other arithmetic  138 us (13%)
  starting transfers between devices  82.5 us (8%)
  matrix products  67.4 us (6%)
  loops' own time  22.1 us (2%)
  between operations  13.9 us (1%)
    ppermute x4, waiting for transfers between devices, from_behind(): lax.ppermute(value, axis, [(source, source + steps) for source in range(f...  350 us
    mul x16, local copies, waits for them, and re-layouts, correlate(): return result.reshape(group_count, 2, 2, width, 2 * width) * (1.0 / depth)  132 us
    scatter x8, other arithmetic, fill_slot(): results.at[slot]  60.2 us
    ppermute x7, starting transfers between devices, on_device(): lax.ppermute(sent, ('chan', 'tm'), [(i, (i + turn) % size) for i in range...  59.9 us
    gather x8, local copies, waits for them, and re-layouts, correlate(): right_rows = jnp.take(full, rows_b, axis=2)  34.7 us
    gather x8, local copies, waits for them, and re-layouts, correlate(): left_rows = jnp.take(full, rows_a, axis=2) * weight  34.6 us
    add x1, other arithmetic, on_device(): filtered + taps_filter[tap_index] * extended[:, :, start:start + frames]....  24.4 us
    all_gather x1, waiting for transfers between devices, on_device(): full = lax.all_gather(arranged, 'pol', axis=1, tiled=True)  23.7 us
  transfers between devices with their start and end apart: 12, of which 8 were waited for; matrix products, arithmetic and copies ran while one was open for 1% of the time, Pallas kernels for 0%

profile of v1, /device:TPU:0, one launch (start us, length us, event | category | flops | bytes accessed | tf_op | source)
XLA Modules:
  0.0 1057.3 jit_solution(4682618853087829630)
XLA Ops:
  18.1 89.9 %collective-permute-done = bf16[2,128,4,2048]{1,3,2,0:T(8,128)(2,1)S(1)} collective-permute-done((bf16[2,128,4,2048]{1,3,2,0:T(8,128)(2,1)}, bf16[2,128,4,2048]{1,3,2,0:T(8,128)(2,1)S(1)}, u32[]{:S(2)}, u32[]{:S(2)}) %collective-permute-start) | collective-permute-done | bytes 4194336 | tf_op jit(solution)/shard_map/ppermute | solution.py:27
  112.5 88.7 %collective-permute-done.1 = bf16[2,128,4,2048]{1,3,2,0:T(8,128)(2,1)S(1)} collective-permute-done((bf16[2,128,4,2048]{1,3,2,0:T(8,128)(2,1)S(1)}, bf16[2,128,4,2048]{1,3,2,0:T(8,128)(2,1)S(1)}, u32[]{:S(2)}, u32[]{:S(2)}) %collective-permute-start.1) | collective-permute-done | bytes 4194336 | tf_op jit(solution)/shard_map/ppermute | solution.py:27
  209.6 86.0 %collective-permute-done.2 = bf16[2,128,4,2048]{1,3,2,0:T(8,128)(2,1)} collective-permute-done((bf16[2,128,4,2048]{1,3,2,0:T(8,128)(2,1)S(1)}, bf16[2,128,4,2048]{1,3,2,0:T(8,128)(2,1)}, u32[]{:S(2)}, u32[]{:S(2)}) %collective-permute-start.2) | collective-permute-done | bytes 4194336 | tf_op jit(solution)/shard_map/ppermute | solution.py:27
  302.3 85.2 %collective-permute-done.3 = bf16[2,128,4,2048]{1,3,2,0:T(8,128)(2,1)} collective-permute-done((bf16[2,128,4,2048]{1,3,2,0:T(8,128)(2,1)}, bf16[2,128,4,2048]{1,3,2,0:T(8,128)(2,1)}, u32[]{:S(2)}, u32[]{:S(2)}) %collective-permute-start.3) | collective-permute-done | bytes 4194336 | tf_op jit(solution)/shard_map/ppermute | solution.py:27
  407.4 24.4 %multiply_add_fusion = f32[2,128,4,2048]{1,3,2,0:T(8,128)} fusion(bf16[2,128,4,2048]{1,3,2,0:T(8,128)(2,1)} %collective-permute-done.2, bf16[2,128,4,2048]{1,3,2,0:T(8,128)(2,1)S(1)} %copy-done.5, bf16[2,128,4,2048]{1,3,2,0:T(8,128)(2,1)} %copy-done.6, bf16[2,128,4,2048]{1,3,2,0:T(8,128)(2,1)} %bitcast.180, bf16[2,128,8,2048]{1,3,2,0:T(8,128)(2,1)} %copy-done.2, ...), kind=kLoop, calls=%fused_computation.44 | loop fusion | flops 104857600 | bytes 63045632 | tf_op jit(solution)/shard_map/add | solution.py:105
  455.8 8.5 fusion.16
  498.9 11.2 %copy.62 = bf16[2,2,4,256,128,4]{3,0,5,4,2,1:T(2,128)(2,1)} copy(bf16[2,2,4,256,128,4]{4,3,2,1,5,0:T(8,128)(2,1)} %fusion.13) | data formatting | bytes 8388608 | tf_op jit(solution)/shard_map/transpose | solution.py:113
  524.5 9.0 collective-permute-done.4
  533.6 23.4 %collective-permute-start.9 = (bf16[1,2,1,256,512]{3,1,4,0,2:T(2,128)(2,1)S(1)}, bf16[1,2,1,256,512]{3,1,4,0,2:T(2,128)(2,1)S(1)}, u32[]{:S(2)}, u32[]{:S(2)}) collective-permute-start(bf16[1,2,1,256,512]{3,1,4,0,2:T(2,128)(2,1)S(1)} %get-tuple-element.119), channel_id=1, source_target_pairs={{0,12},{2,14},{4,0},{6,2},{8,4},{10,6},{12,8},{14,10},{1,13},{3,15... | collective-permute-start | bytes 1572872 | tf_op jit(solution)/shard_map/ppermute | solution.py:121
  559.1 26.8 %collective-permute-start.10 = (bf16[1,2,1,256,512]{3,1,4,0,2:T(2,128)(2,1)S(1)}, bf16[1,2,1,256,512]{3,1,4,0,2:T(2,128)(2,1)S(1)}, u32[]{:S(2)}, u32[]{:S(2)}) collective-permute-start(bf16[1,2,1,256,512]{3,1,4,0,2:T(2,128)(2,1)S(1)} %get-tuple-element.118), channel_id=1, source_target_pairs={{0,14},{2,0},{4,2},{6,4},{8,6},{10,8},{12,10},{14,12},{1,15},{3,1}... | collective-permute-start | bytes 1572872 | tf_op jit(solution)/shard_map/ppermute | solution.py:121
  601.6 19.8 %copy.63 = bf16[2,2,128,256,4,4]{2,1,5,4,3,0:T(2,128)(2,1)} copy(bf16[2,2,128,256,4,4]{3,0,5,2,4,1:T(2,128)(2,1)} %bitcast.176) | data formatting | bytes 8388608 | tf_op jit(solution)/shard_map/transpose | solution.py:130
  629.0 7.8 copy.64
  639.7 23.7 %all-gather.2.cloned.1.call-done = bf16[2,2,256,32,128]{4,3,2,0,1:T(8,128)(2,1)} async-done(((bf16[2,1,256,32,128]{4,3,2,0,1:T(8,128)(2,1)}), bf16[2,2,256,32,128]{4,3,2,0,1:T(8,128)(2,1)}) %all-gather.2.cloned.1.call-update) | async-done | bytes 8388624 | tf_op jit(solution)/shard_map/all_gather | solution.py:133
  663.4 8.4 copy.65
  671.8 11.5 %broadcast_in_dim.13 = f32[8,32,2,2,64,128]{5,4,3,2,1,0:T(8,128)} broadcast(f32[]{:T(128)} %constant.207.clone.1), dimensions={} | broadcast | bytes 33554436 | tf_op jit(solution)/shard_map/broadcast_in_dim | solution.py:140
  683.3 366.9 %while.11 = (s32[]{:T(128)}, f32[8,32,2,2,64,128]{5,4,3,2,1,0:T(8,128)}, s32[]{:T(128)}, s32[8]{0:T(128)S(1)}, s32[14,64]{1,0:T(8,128)}, /*index=5*/bf16[2,2,256...) while((s32[]{:T(128)}, ...), condition=%wide.region_6.8_spmd, body=%wide.region_4.7_spmd.sunk | while | flops 563612416 | bytes 78656224 | solution.py:150
  712.9 8.8 mul.778
  758.7 8.8 mul.778
  804.5 8.8 mul.778
  850.2 8.8 mul.778
  896.0 8.8 mul.778
  941.7 8.8 mul.778
  987.5 8.8 mul.778
  1033.3 8.8 mul.778
  (246 shorter events, 426.5 us)
Async XLA Ops:
  6.5 295.6 %copy-start.7 = (f32[16,2048]{1,0:T(8,128)S(1)}, f32[16,2048]{1,0:T(8,128)}, u32[]{:S(2)}) copy-start(f32[16,2048]{1,0:T(8,128)} %param.13) | copy-start | bytes 393220
  6.5 656.8 %all-gather.2.cloned.1.call-start = ((), (), s32[]{:S(2)}) async-start(), calls=%async_computation | async-start | bytes 12582912 | tf_op jit(solution)/shard_map/all_gather | solution.py:133
  12.9 95.1 %collective-permute-start = (bf16[2,128,4,2048]{1,3,2,0:T(8,128)(2,1)}, bf16[2,128,4,2048]{1,3,2,0:T(8,128)(2,1)S(1)}, u32[]{:S(2)}, u32[]{:S(2)}) collective-permute-start(bf16[2,128,4,2048]{1,3,2,0:T(8,128)(2,1)} %bitcast.179), channel_id=1, source_target_pairs={{0,2},{2,4},{4,6},{1,3},{3,5},{5,7},{8,10},{10,12},{12,14},{9,11},... | collective-permute-start | bytes 12582920 | tf_op jit(solution)/shard_map/ppermute | solution.py:27
  108.0 187.6 %copy-start.6 = (bf16[2,128,4,2048]{1,3,2,0:T(8,128)(2,1)}, bf16[2,128,4,2048]{1,3,2,0:T(8,128)(2,1)S(1)}, u32[]{:S(2)}) copy-start(bf16[2,128,4,2048]{1,3,2,0:T(8,128)(2,1)S(1)} %collective-permute-done) | copy-start | bytes 12582916
  108.0 93.2 %collective-permute-start.1 = (bf16[2,128,4,2048]{1,3,2,0:T(8,128)(2,1)S(1)}, bf16[2,128,4,2048]{1,3,2,0:T(8,128)(2,1)S(1)}, u32[]{:S(2)}, u32[]{:S(2)}) collective-permute-start(bf16[2,128,4,2048]{1,3,2,0:T(8,128)(2,1)S(1)} %collective-permute-done), channel_id=1, source_target_pairs={{0,2},{2,4},{4,6},{1,3},{3,5},{5,7},{8,10},{10,12},{12,14},{9,11},... | collective-permute-start | bytes 12582920 | tf_op jit(solution)/shard_map/ppermute | solution.py:27
  201.2 1.9 copy-start.4
  203.1 92.4 %collective-permute-start.2 = (bf16[2,128,4,2048]{1,3,2,0:T(8,128)(2,1)S(1)}, bf16[2,128,4,2048]{1,3,2,0:T(8,128)(2,1)}, u32[]{:S(2)}, u32[]{:S(2)}) collective-permute-start(bf16[2,128,4,2048]{1,3,2,0:T(8,128)(2,1)S(1)} %collective-permute-done.1), channel_id=1, source_target_pairs={{0,2},{2,4},{4,6},{1,3},{3,5},{5,7},{8,10},{10,12},{12,14},{9,11},... | collective-permute-start | bytes 12582920 | tf_op jit(solution)/shard_map/ppermute | solution.py:27
  295.5 91.9 %collective-permute-start.3 = (bf16[2,128,4,2048]{1,3,2,0:T(8,128)(2,1)}, bf16[2,128,4,2048]{1,3,2,0:T(8,128)(2,1)}, u32[]{:S(2)}, u32[]{:S(2)}) collective-permute-start(bf16[2,128,4,2048]{1,3,2,0:T(8,128)(2,1)} %collective-permute-done.2), channel_id=1, source_target_pairs={{0,2},{2,4},{4,6},{1,3},{3,5},{5,7},{8,10},{10,12},{12,14},{9,11},... | collective-permute-start | bytes 12582920 | tf_op jit(solution)/shard_map/ppermute | solution.py:27
  389.9 7.1 copy-start.5
  393.6 3.4 copy-start.2
  398.4 5.8 copy-start
  404.2 3.2 copy-start.1
  514.8 18.7 %collective-permute-start.4 = (bf16[1,2,1,256,512]{3,1,4,0,2:T(2,128)(2,1)}, bf16[1,2,1,256,512]{3,1,4,0,2:T(2,128)(2,1)}, u32[]{:S(2)}, u32[]{:S(2)}) collective-permute-start(bf16[1,2,1,256,512]{3,1,4,0,2:T(2,128)(2,1)} %get-tuple-element.124), channel_id=1, source_target_pairs={{0,2},{2,4},{4,6},{6,8},{8,10},{10,12},{12,14},{14,0},{1,3},{3,5},... | collective-permute-start | bytes 1572872 | tf_op jit(solution)/shard_map/ppermute | solution.py:121
  517.3 41.8 %collective-permute-start.5 = (bf16[1,2,1,256,512]{3,1,4,0,2:T(2,128)(2,1)S(1)}, bf16[1,2,1,256,512]{3,1,4,0,2:T(2,128)(2,1)}, u32[]{:S(2)}, u32[]{:S(2)}) collective-permute-start(bf16[1,2,1,256,512]{3,1,4,0,2:T(2,128)(2,1)S(1)} %get-tuple-element.123), channel_id=1, source_target_pairs={{0,4},{2,6},{4,8},{6,10},{8,12},{10,14},{12,0},{14,2},{1,5},{3,7},... | collective-permute-start | bytes 1572872 | tf_op jit(solution)/shard_map/ppermute | solution.py:121
  520.1 68.0 %collective-permute-start.6 = (bf16[1,2,1,256,512]{3,1,4,0,2:T(2,128)(2,1)S(1)}, bf16[1,2,1,256,512]{3,1,4,0,2:T(2,128)(2,1)}, u32[]{:S(2)}, u32[]{:S(2)}) collective-permute-start(bf16[1,2,1,256,512]{3,1,4,0,2:T(2,128)(2,1)S(1)} %get-tuple-element.122), channel_id=1, source_target_pairs={{0,6},{2,8},{4,10},{6,12},{8,14},{10,0},{12,2},{14,4},{1,7},{3,9},... | collective-permute-start | bytes 1572872 | tf_op jit(solution)/shard_map/ppermute | solution.py:121
  522.4 67.9 %collective-permute-start.7 = (bf16[1,2,1,256,512]{3,1,4,0,2:T(2,128)(2,1)S(1)}, bf16[1,2,1,256,512]{3,1,4,0,2:T(2,128)(2,1)}, u32[]{:S(2)}, u32[]{:S(2)}) collective-permute-start(bf16[1,2,1,256,512]{3,1,4,0,2:T(2,128)(2,1)S(1)} %get-tuple-element.121), channel_id=1, source_target_pairs={{0,8},{2,10},{4,12},{6,14},{8,0},{10,2},{12,4},{14,6},{1,9},{3,11}... | collective-permute-start | bytes 1572872 | tf_op jit(solution)/shard_map/ppermute | solution.py:121
  522.9 69.6 %collective-permute-start.8 = (bf16[1,2,1,256,512]{3,1,4,0,2:T(2,128)(2,1)S(1)}, bf16[1,2,1,256,512]{3,1,4,0,2:T(2,128)(2,1)}, u32[]{:S(2)}, u32[]{:S(2)}) collective-permute-start(bf16[1,2,1,256,512]{3,1,4,0,2:T(2,128)(2,1)S(1)} %get-tuple-element.120), channel_id=1, source_target_pairs={{0,10},{2,12},{4,14},{6,0},{8,2},{10,4},{12,6},{14,8},{1,11},{3,13... | collective-permute-start | bytes 1572872 | tf_op jit(solution)/shard_map/ppermute | solution.py:121
  533.6 61.9 %collective-permute-start.9 = (bf16[1,2,1,256,512]{3,1,4,0,2:T(2,128)(2,1)S(1)}, bf16[1,2,1,256,512]{3,1,4,0,2:T(2,128)(2,1)S(1)}, u32[]{:S(2)}, u32[]{:S(2)}) collective-permute-start(bf16[1,2,1,256,512]{3,1,4,0,2:T(2,128)(2,1)S(1)} %get-tuple-element.119), channel_id=1, source_target_pairs={{0,12},{2,14},{4,0},{6,2},{8,4},{10,6},{12,8},{14,10},{1,13},{3,15... | collective-permute-start | bytes 1572872 | tf_op jit(solution)/shard_map/ppermute | solution.py:121
  559.1 41.3 %collective-permute-start.10 = (bf16[1,2,1,256,512]{3,1,4,0,2:T(2,128)(2,1)S(1)}, bf16[1,2,1,256,512]{3,1,4,0,2:T(2,128)(2,1)S(1)}, u32[]{:S(2)}, u32[]{:S(2)}) collective-permute-start(bf16[1,2,1,256,512]{3,1,4,0,2:T(2,128)(2,1)S(1)} %get-tuple-element.118), channel_id=1, source_target_pairs={{0,14},{2,0},{4,2},{6,4},{8,6},{10,8},{12,10},{14,12},{1,15},{3,1}... | collective-permute-start | bytes 1572872 | tf_op jit(solution)/shard_map/ppermute | solution.py:121
  671.8 11.5 %copy-start.9 = (s32[6]{0:T(128)S(1)}, s32[6]{0:T(128)}, u32[]{:S(2)}) copy-start(s32[6]{0:T(128)} %constant.202.clone.1) | copy-start | bytes 76
  702.5 1.2 copy-start.3
  748.3 1.2 copy-start.3
  885.5 1.2 copy-start.3
  1022.8 1.2 copy-start.3
  (5 other events, 5.6 us)
Sparse Core Ops, SparseCore 0:
  637.0 26.3 all-gather.1
